TPU v7x, 128 devices: a whole 4x4x4 slice. The times are simulated.
128 devices in a mesh: row: 16 (over y, z_lo, core), col: 8 (over x, z_hi).
Axes of the slice: x: 4, y: 4, z: 4 (z_hi: 2, z_lo: 2; z = z_hi * 2 + z_lo), core: 2. Of those that a mesh axis runs over, the one named last changes fastest.
Arguments:
- pair: bfloat16 [768, 768, 128], P('row', 'col'), may hold values from -6 to 6
- bins: int32 [768, 768], P('row', 'col'), may hold values from 0 to 14
- mask: int32 [768], replicated, may hold values 0 or 1
- emb_table: bfloat16 [15, 128], replicated, may hold values from -6 to 6
- ln_gain: float32 [128], replicated, may hold values from 0.1 to 1.9
- ln_bias: float32 [128], replicated, may hold values from -3 to 3
- proj_weight: bfloat16 [128, 512], replicated, may hold values from -0.5 to 0.5
- gate_weight: bfloat16 [128, 128], replicated, may hold values from -0.5 to 0.5
- norm_gain: float32 [128], replicated, may hold values from 0.1 to 1.9
- norm_bias: float32 [128], replicated, may hold values from -3 to 3
- out_weight: bfloat16 [128, 128], replicated, may hold values from -0.5 to 0.5
Outputs:
- pair_out: bfloat16 [768, 768, 128], P('row', 'col')
All inputs are finite; a program needn't handle non-finite values.
Results may differ from a plain program's by a relative error of at most 0.0085.
Values may be sent and summed in bfloat16 or wider, within the bound.
No kernel may reach another device: no remote copies, remote signals or barrier semaphores. Data moves between devices by JAX's collectives and lax.ppermute only.
A program may use at most 128 MiB of HBM per device.

v0:
```python
import jax
import jax.numpy as jnp
from jax import lax
from jax.experimental import pallas as pl
from jax.experimental.pallas import tpu as pltpu
from jax.sharding import PartitionSpec as P

EPS = 1e-5
F32 = jnp.float32
BF16 = jnp.bfloat16
I32 = jnp.int32
NT = (((1,), (1,)), ((), ()))
TN = (((0,), (0,)), ((), ()))
NN = (((1,), (0,)), ((), ()))
LIMIT = 24 * 1024 * 1024
IN_HBM = pl.BlockSpec(memory_space=pltpu.HBM)
IN_VMEM = pl.BlockSpec(memory_space=pltpu.VMEM)


def column_row(col, entry):
    if col < 8:
        return 8 * entry + col
    return 32 + 8 * (entry % 2) + 4 * (entry // 2) + col - 8


def lanes_slot(shape):
    return lax.broadcasted_iota(I32, shape, len(shape) - 1) // 32


def pick(entry, parts):
    got = parts[0]
    for e in range(1, 4):
        got = jnp.where(entry == e, parts[e], got)
    return got


def sigmoid(x):
    return 0.5 * jnp.tanh(0.5 * x) + 0.5


def norm_sublanes(x, gain, bias):
    mean = jnp.mean(x, axis=0, keepdims=True)
    centred = x - mean
    var = jnp.mean(centred * centred, axis=0, keepdims=True)
    scaled = centred * lax.rsqrt(var + EPS)
    return [scaled[:, n : n + 128] * gain + bias for n in range(0, x.shape[1], 128)]


def in_hbm(*arrays):
    return [pltpu.with_memory_space_constraint(a, pltpu.HBM) for a in arrays]


def dot(a, b, dims=NN):
    return lax.dot_general(a, b, dims, preferred_element_type=F32)


def down(row):
    return jnp.broadcast_to(row, (128, 128)).T


def eye128():
    rows = lax.broadcasted_iota(I32, (128, 128), 0)
    cols = lax.broadcasted_iota(I32, (128, 128), 1)
    return jnp.where(rows == cols, 1.0, 0.0).astype(BF16)


def padded(emb):
    return jnp.concatenate([emb.astype(F32), jnp.zeros((1, 128), F32)], axis=0)


def columns(codes, shift, rot):
    entry = (lanes_slot((8, 128)) + 4 - rot) % 4
    turn = lambda x, e: pltpu.roll(x, 32 * ((e + shift) % 4), 1)
    head = pick(entry, [turn(codes[8 * b : 8 * b + 8, :], b) for b in range(4)])
    ends = [turn(codes[32 + 8 * (e % 2) : 40 + 8 * (e % 2), :], e) for e in range(4)]
    tail = pick(entry[:4], [ends[0][:4], ends[1][:4], ends[2][4:], ends[3][4:]])
    return [head[c : c + 1, :] for c in range(8)] + [tail[c : c + 1, :] for c in range(4)]


def one_hot(codes):
    level = lax.broadcasted_iota(I32, (16, codes.shape[1]), 0)
    return jnp.where((codes & 15) == level, 1.0, 0.0).astype(BF16)


def half_columns(half):
    return [2 * half, 2 * half + 1, 2 * half + 4, 2 * half + 5, 8 + 2 * half, 9 + 2 * half]


def project_kernel(
    mask_h, pair_h, bins_h, emb_h, gain_h, bias_h, weight_h, out, normed_out, codes_out,
    mask, pair, bins, emb, gain, bias, weight, code, normed, done, sems,
):
    r, q = lax.axis_index("row"), lax.axis_index("col")
    small = [
        pltpu.make_async_copy(a, b, sems.at[n])
        for n, (a, b) in enumerate(
            ((mask_h, mask), (weight_h, weight), (gain_h, gain), (bias_h, bias), (emb_h, emb), (bins_h, bins))
        )
    ]
    large = []
    for m in range(3):
        at = (slice(None), pl.ds(32 * m, 32))
        large.append(pltpu.make_async_copy(pair_h.at[at], pair.at[at], sems.at[6 + m]))
    for copy in small + large:
        copy.start()
    for copy in small[:4]:
        copy.wait()

    weight_t = (0.5 * weight[...].astype(F32)).T.astype(BF16)
    gain_t, bias_t = down(gain[...]), down(bias[...])
    lane = lax.broadcasted_iota(I32, (8, 128), 1)
    sub = lax.broadcasted_iota(I32, (8, 128), 0)
    along = [jnp.zeros((8, 128), I32) for _ in range(4)]
    for k in range(96):
        along[k % 4] = jnp.where(lane == k, mask[96 * q + k], along[k % 4])
    along = 16 * (along[0] + along[1] + along[2] + along[3])
    for b in range(6):
        across = jnp.zeros((8, 128), I32)
        for g in range(8):
            across = jnp.where(sub == g, mask[48 * r + 8 * b + g], across)
        code[8 * b : 8 * b + 8, :] = across * along
    for copy in small[4:]:
        copy.wait()
    emb_t = padded(emb[...]).T.astype(BF16)
    code[:, :96] = code[:, :96] + bins[...]
    eye = eye128()
    for copy in large:
        copy.wait()
    for m in range(3):
        rot = (3 * q + m) % 4
        codes = columns(code, 3 * q, rot)
        codes_out[m] = jnp.concatenate(codes, axis=0)
        codes = jnp.concatenate(codes, axis=1)
        rows = [
            pair[column_row(c, (s + 4 - rot) % 4), 32 * m : 32 * m + 32]
            for c in range(12)
            for s in range(4)
        ]
        x = jnp.concatenate(rows, axis=0)
        summed = dot(eye, x, NT) + dot(emb_t, one_hot(codes))
        parts = jnp.concatenate(norm_sublanes(summed, gain_t, bias_t), axis=1)
        normed_out[:, 1536 * m : 1536 * (m + 1)] = parts.astype(BF16)
        normed[:, 1536 * m : 1536 * (m + 1)] = jnp.where(codes >= 16, parts, 0.0).astype(BF16)

    for m in range(3):
        low = (lanes_slot((128, 128)) + 4 - (3 * q + m) % 4) % 4 < 2
        sides = []
        for side in range(2):
            proj = dot(
                weight_t[256 * side : 256 * (side + 1)], normed[:, 1536 * m : 1536 * (m + 1)]
            )
            value, gate = proj[:128], proj[128:]
            sides.append((jnp.tanh(gate) + 1.0) * value)
        left, right = sides
        for g in range(8):
            own = slice(128 * g, 128 * (g + 1))
            end = slice(128 * (8 + g % 4), 128 * (9 + g % 4))
            left_end, right_end = left[:, end], right[:, end]
            if g < 4:
                left_end = pltpu.roll(left_end, 64, 1)
            else:
                right_end = pltpu.roll(right_end, 64, 1)
            done[24 * m + g] = left[:, own].astype(BF16)
            done[24 * m + 8 + g] = jnp.where(low, right[:, own], left_end).astype(BF16)
            done[24 * m + 16 + g] = jnp.where(low, right_end, right[:, own]).astype(BF16)
    out[...] = jnp.swapaxes(done[...], 0, 1)


def project(mask, pair, bins, emb, gain, bias, weight):
    return pl.pallas_call(
        project_kernel,
        in_specs=[IN_HBM] * 7,
        out_specs=[IN_VMEM] * 3,
        out_shape=[
            jax.ShapeDtypeStruct((128, 72, 128), BF16),
            jax.ShapeDtypeStruct((128, 4608), BF16),
            jax.ShapeDtypeStruct((3, 12, 128), I32),
        ],
        scratch_shapes=[
            pltpu.SMEM((768,), I32),
            pltpu.VMEM((48, 96, 128), BF16),
            pltpu.VMEM((48, 96), I32),
            pltpu.VMEM((15, 128), BF16),
            pltpu.VMEM((1, 128), F32),
            pltpu.VMEM((1, 128), F32),
            pltpu.VMEM((128, 512), BF16),
            pltpu.VMEM((48, 128), I32),
            pltpu.VMEM((128, 4608), BF16),
            pltpu.VMEM((72, 128, 128), BF16),
            pltpu.SemaphoreType.DMA((9,)),
        ],
        compiler_params=pltpu.CompilerParams(vmem_limit_bytes=LIMIT),
        name="project",
    )(*in_hbm(mask, pair, bins, emb, gain, bias, weight))


LEFT_AT = [(0, 0), (0, 1), (0, 2), (0, 3), (1, 2), (1, 3)]
RIGHT_AT = [(1, 0), (1, 1), (2, 2), (2, 3), (2, 0), (2, 1)]


def roll_slots(x, by):
    by %= 4
    return x if by == 0 else pltpu.roll(x, 32 * by, 1)


def triangle_kernel(recv, out, left, right, tri):
    slot = lanes_slot((8, 128))

    def gather(r, places, dest):
        for tile in range(6):
            src = []
            for z in range(4):
                q, m = divmod(4 * tile + z, 3)
                src.append(recv[8 * r + q, 24 * m : 24 * (m + 1)].astype(F32))
            got = []
            for h, e in places:
                merged = pick((slot + 4 - e) % 4, [v[8 * h : 8 * (h + 1)] for v in src])
                got.append(roll_slots(merged, -e))
            dest[48 * r : 48 * r + 48, 128 * tile : 128 * (tile + 1)] = (
                jnp.concatenate(got, axis=0).astype(BF16)
            )

    def scatter(r):
        full, ends = {}, {}
        for tile in range(6):
            cols = slice(128 * tile, 128 * (tile + 1))
            piece = [tri[48 * r + 8 * b : 48 * r + 8 * b + 8, cols] for b in range(6)]
            head = [roll_slots(piece[b], b) for b in range(4)]
            tail = [roll_slots(piece[4 + e % 2], e) for e in range(4)]
            tail = [tail[0][:4], tail[1][:4], tail[2][4:], tail[3][4:]]
            for z in range(4):
                entry = (slot + 4 - z) % 4
                full[4 * tile + z] = pick(entry, head)
                ends[4 * tile + z] = pick(entry[:4], tail)
        for q in range(8):
            heads = [full[3 * q + m] for m in range(3)]
            parts = [v[at : at + 4] for v in heads for at in (0, 4)]
            parts += [ends[3 * q + m] for m in range(3)]
            out[8 * r + q] = jnp.concatenate(parts, axis=1).astype(BF16)

    for r in range(16):
        gather(r, RIGHT_AT, right)
        gather(r, LEFT_AT, left)
    tri[...] = dot(left[...], right[...], NT)
    for r in range(16):
        scatter(r)


def triangle(recv):
    return pl.pallas_call(
        triangle_kernel,
        in_specs=[IN_VMEM],
        out_specs=IN_VMEM,
        out_shape=jax.ShapeDtypeStruct((128, 4, 1152), BF16),
        scratch_shapes=[
            pltpu.VMEM((768, 768), BF16),
            pltpu.VMEM((768, 768), BF16),
            pltpu.VMEM((768, 768), F32),
        ],
        compiler_params=pltpu.CompilerParams(vmem_limit_bytes=LIMIT),
        name="triangle",
    )(recv)


def update_kernel(
    tri, normed, codes, pair, emb, gain, bias, gate_weight, out_weight, out, sums, result, sems
):
    q = lax.axis_index("col")
    gain_t, bias_t = down(gain[...]), down(bias[...])
    zeros = jnp.zeros((128, 128), BF16)
    both = jnp.concatenate(
        [
            jnp.concatenate([(0.5 * gate_weight[...].astype(F32)).astype(BF16), zeros], axis=1),
            jnp.concatenate([zeros[:16], padded(emb[...]).astype(BF16)], axis=1),
        ],
        axis=0,
    )
    for u in range(9):
        part = tri[:, :, 128 * u : 128 * (u + 1)].astype(F32)
        sums[4 * u : 4 * u + 4] = jnp.swapaxes(part, 0, 1).astype(BF16)
    stores = []
    for m in range(3):
        rot = (3 * q + m) % 4
        at = slice(32 * m, 32 * m + 32)
        hot = one_hot(jnp.concatenate([codes[m, c : c + 1, :] for c in range(12)], axis=1))
        lanes = slice(1536 * m, 1536 * (m + 1))
        mixed = dot(jnp.concatenate([normed[:, lanes], hot], axis=0), both, TN)
        x = [sums[8 * m + c if c < 8 else 16 + 4 * m + c].astype(F32) for c in range(12)]
        tri_normed = norm_sublanes(jnp.concatenate(x, axis=1), gain_t, bias_t)
        change = dot(jnp.concatenate(tri_normed, axis=1).astype(BF16), out_weight[...], TN)
        change = (0.5 * jnp.tanh(mixed[:, :128]) + 0.5) * change
        for c in range(12):
            for s in range(4):
                i = column_row(c, (s + 4 - rot) % 4)
                k = slice(128 * c + 32 * s, 128 * c + 32 * s + 32)
                total = pair[i, at].astype(F32) + mixed[k, 128:]
                result[i, at] = (total + change[k]).astype(BF16)
        part = (slice(None), pl.ds(32 * m, 32))
        stores.append(pltpu.make_async_copy(result.at[part], out.at[part], sems.at[m]))
        stores[m].start()
    for store in stores:
        store.wait()


def update(*args):
    return pl.pallas_call(
        update_kernel,
        in_specs=[IN_VMEM] * 9,
        out_specs=IN_HBM,
        out_shape=jax.ShapeDtypeStruct((48, 96, 128), BF16),
        scratch_shapes=[
            pltpu.VMEM((36, 128, 128), BF16),
            pltpu.VMEM((48, 96, 128), BF16),
            pltpu.SemaphoreType.DMA((3,)),
        ],
        compiler_params=pltpu.CompilerParams(vmem_limit_bytes=LIMIT),
        name="update",
    )(*args)


def body(
    pair,
    bins,
    mask,
    emb_table,
    ln_gain,
    ln_bias,
    proj_weight,
    gate_weight,
    norm_gain,
    norm_bias,
    out_weight,
):
    row = lambda v: v.reshape(1, 128)
    sides, normed, codes = project(
        mask, pair, bins, emb_table, row(ln_gain), row(ln_bias), proj_weight
    )
    recv = lax.all_to_all(sides, ("row", "col"), 0, 0, tiled=True)
    tri = lax.all_to_all(triangle(recv), ("row", "col"), 0, 0, tiled=True)
    return update(
        tri, normed, codes, pair, emb_table, row(norm_gain), row(norm_bias), gate_weight, out_weight
    )


def solution(mesh):
    placed = (P("row", "col", None), P("row", "col"), P(), P(), P(), P(), P(), P(), P(), P(), P())
    return jax.shard_map(
        body, mesh=mesh, in_specs=placed, out_specs=P("row", "col", None), check_vma=False
    )
```

profile of v0, /device:TPU:1, one launch (start us, length us, event | category | flops | bytes accessed | tf_op | source)
XLA Modules:
  0.0 79.5 jit_solution(2006296778524576353)
XLA Ops:
  0.0 3.8 %project.1 = (bf16[128,72,128]{2,1,0:T(8,128)(2,1)S(1)}, bf16[128,4608]{1,0:T(8,128)(2,1)S(1)}, s32[3,12,128]{2,1,0:T(8,128)S(1)}) custom-call(s32[768]{0:T(1024)} %mask_h.1, bf16[48,96,128]{2,1,0:T(8,128)(2,1)} %pair.1, s32[48,96]{1,0:T(8,128)} %bins_h.1, bf16[15,128]{1,0:T(8,128)(2,1)} %emb.1, f32[1,128]{1,0:T(1,128)} %bitcast.6, f32[1,128]{1,0:T(1,128)} %bitcast.7, ...), custom_call_target="tpu_custom_call" | custom-call | tf_op jit(solution)/shard_map/project/pallas_call | solution.py:170
  3.8 44.7 %all_to_all.10.recv = bf16[128,72,128]{2,1,0:T(8,128)(2,1)S(1)} all-to-all(bf16[128,72,128]{2,1,0:T(8,128)(2,1)S(1)} %get-tuple-element.8), channel_id=1, replica_groups=mesh['row'=16,'col'=8] {'row','col'}, dimensions={0} | all-to-all | bytes 4718592 | tf_op jit(solution)/shard_map/all_to_all | solution.py:338
  48.5 2.4 %triangle.1 = bf16[128,4,1152]{2,1,0:T(4,128)(2,1)S(1)} custom-call(bf16[128,72,128]{2,1,0:T(8,128)(2,1)S(1)} %all_to_all.10.recv), custom_call_target="tpu_custom_call" | custom-call | tf_op jit(solution)/shard_map/triangle/pallas_call | solution.py:250
  50.9 0.0 copy-start
  50.9 0.0 copy-start.1
  50.9 0.0 copy-start.2
  50.9 0.0 copy-start.3
  50.9 0.0 copy-start.4
  50.9 0.0 copy-start.5
  51.0 25.1 %all_to_all.11.tri = bf16[128,4,1152]{2,1,0:T(4,128)(2,1)S(1)} all-to-all(bf16[128,4,1152]{2,1,0:T(4,128)(2,1)S(1)} %triangle.1), channel_id=1, replica_groups=mesh['row'=16,'col'=8] {'row','col'}, dimensions={0} | all-to-all | bytes 2359296 | tf_op jit(solution)/shard_map/all_to_all | solution.py:339
  76.0 0.0 copy-done
  76.0 0.0 copy-done.1
  76.0 0.0 copy-done.2
  76.0 0.0 copy-done.3
  76.0 0.0 copy-done.4
  76.1 0.0 copy-done.5
  76.1 3.4 %update.1 = bf16[48,96,128]{2,1,0:T(8,128)(2,1)} custom-call(bf16[128,4,1152]{2,1,0:T(4,128)(2,1)S(1)} %all_to_all.11.tri, bf16[128,4608]{1,0:T(8,128)(2,1)S(1)} %get-tuple-element.9.normed, s32[3,12,128]{2,1,0:T(8,128)S(1)} %get-tuple-element.10.codes, bf16[48,96,128]{2,1,0:T(8,128)(2,1)S(1)} %copy-done, bf16[15,128]{1,0:T(8,128)(2,1)S(1)} %copy-done.3, ...), custom_call_target="tpu_custom_call" | custom-call | tf_op jit(solution)/shard_map/update/pallas_call | solution.py:306
Async XLA Ops:
  50.9 25.1 %copy-start = (bf16[48,96,128]{2,1,0:T(8,128)(2,1)S(1)}, bf16[48,96,128]{2,1,0:T(8,128)(2,1)}, u32[]{:S(2)}) copy-start(bf16[48,96,128]{2,1,0:T(8,128)(2,1)} %pair.1) | copy-start | bytes 3538948
  50.9 25.1 %copy-start.1 = (bf16[128,128]{1,0:T(8,128)(2,1)S(1)}, bf16[128,128]{1,0:T(8,128)(2,1)}, u32[]{:S(2)}) copy-start(bf16[128,128]{1,0:T(8,128)(2,1)} %gate_weight.1) | copy-start | bytes 98308
  50.9 25.1 %copy-start.2 = (bf16[128,128]{1,0:T(8,128)(2,1)S(1)}, bf16[128,128]{1,0:T(8,128)(2,1)}, u32[]{:S(2)}) copy-start(bf16[128,128]{1,0:T(8,128)(2,1)} %out_weight.1) | copy-start | bytes 98308
  50.9 25.1 %copy-start.3 = (bf16[15,128]{1,0:T(8,128)(2,1)S(1)}, bf16[15,128]{1,0:T(8,128)(2,1)}, u32[]{:S(2)}) copy-start(bf16[15,128]{1,0:T(8,128)(2,1)} %emb.1) | copy-start | bytes 11524
  50.9 25.1 %copy-start.4 = (f32[128]{0:T(128)S(1)}, f32[128]{0:T(128)}, u32[]{:S(2)}) copy-start(f32[128]{0:T(128)} %param.19) | copy-start | bytes 1540
  50.9 25.1 %copy-start.5 = (f32[128]{0:T(128)S(1)}, f32[128]{0:T(128)}, u32[]{:S(2)}) copy-start(f32[128]{0:T(128)} %param.20) | copy-start | bytes 1540
where the time goes:
time: 79.6 us; the launch traced here: 79.5 us
  blocking collectives  69.8 us (88%)
  Pallas kernels  9.54 us (12%)
    all_to_all x1, blocking collectives, body(): recv = lax.all_to_all(sides, ('row', 'col'), 0, 0, tiled=True)  44.7 us
    all_to_all x1, blocking collectives, body(): tri = lax.all_to_all(triangle(recv), ('row', 'col'), 0, 0, tiled=True)  25.1 us
    pallas_call x1, Pallas kernels, project(): pl.pallas_call(project_kernel, in_specs=[IN_HBM] * 7, out_specs=[IN_VMEM]...  3.77 us
    pallas_call x1, Pallas kernels, update(): pl.pallas_call(update_kernel, in_specs=[IN_VMEM] * 9, out_specs=IN_HBM, o...  3.4 us
    pallas_call x1, Pallas kernels, triangle(): pl.pallas_call(triangle_kernel, in_specs=[IN_VMEM], out_specs=IN_VMEM, ou...  2.37 us

commit v1 on v0

--- a/solution.py
+++ b/solution.py
@@ -277,7 +277,7 @@
     )
     for u in range(9):
         part = tri[:, :, 128 * u : 128 * (u + 1)].astype(F32)
-        sums[4 * u : 4 * u + 4] = jnp.swapaxes(part, 0, 1).astype(BF16)
+        sums[512 * u : 512 * (u + 1)] = part.reshape(512, 128)
     stores = []
     for m in range(3):
         rot = (3 * q + m) % 4
@@ -285,7 +285,10 @@
         hot = one_hot(jnp.concatenate([codes[m, c : c + 1, :] for c in range(12)], axis=1))
         lanes = slice(1536 * m, 1536 * (m + 1))
         mixed = dot(jnp.concatenate([normed[:, lanes], hot], axis=0), both, TN)
-        x = [sums[8 * m + c if c < 8 else 16 + 4 * m + c].astype(F32) for c in range(12)]
+        x = []
+        for c in range(12):
+            u, v = divmod(8 * m + c if c < 8 else 16 + 4 * m + c, 4)
+            x.append(sums[pl.ds(512 * u + v, 128, stride=4), :])
         tri_normed = norm_sublanes(jnp.concatenate(x, axis=1), gain_t, bias_t)
         change = dot(jnp.concatenate(tri_normed, axis=1).astype(BF16), out_weight[...], TN)
         change = (0.5 * jnp.tanh(mixed[:, :128]) + 0.5) * change
@@ -309,7 +312,7 @@
         out_specs=IN_HBM,
         out_shape=jax.ShapeDtypeStruct((48, 96, 128), BF16),
         scratch_shapes=[
-            pltpu.VMEM((36, 128, 128), BF16),
+            pltpu.VMEM((4608, 128), F32),
             pltpu.VMEM((48, 96, 128), BF16),
             pltpu.SemaphoreType.DMA((3,)),
         ],

time: 79.6 us -> 79.2 us (level)
  no operation moved by 1% of the time
where the time goes in v1:
time: 79.2 us; the launch traced here: 79.1 us
  blocking collectives  69.8 us (88%)
  Pallas kernels  9.12 us (12%)
    all_to_all x1, blocking collectives, body(): recv = lax.all_to_all(sides, ('row', 'col'), 0, 0, tiled=True)  44.7 us
    all_to_all x1, blocking collectives, body(): tri = lax.all_to_all(triangle(recv), ('row', 'col'), 0, 0, tiled=True)  25.1 us
    pallas_call x1, Pallas kernels, project(): pl.pallas_call(project_kernel, in_specs=[IN_HBM] * 7, out_specs=[IN_VMEM]...  3.77 us
    pallas_call x1, Pallas kernels, update(): pl.pallas_call(update_kernel, in_specs=[IN_VMEM] * 9, out_specs=IN_HBM, o...  2.98 us
    pallas_call x1, Pallas kernels, triangle(): pl.pallas_call(triangle_kernel, in_specs=[IN_VMEM], out_specs=IN_VMEM, ou...  2.37 us

profile of v1, /device:TPU:1, one launch (start us, length us, event | category | flops | bytes accessed | tf_op | source)
XLA Modules:
  0.0 79.1 jit_solution(9237973737883661983)
XLA Ops:
  0.0 3.8 %project.1 = (bf16[128,72,128]{2,1,0:T(8,128)(2,1)S(1)}, bf16[128,4608]{1,0:T(8,128)(2,1)S(1)}, s32[3,12,128]{2,1,0:T(8,128)S(1)}) custom-call(s32[768]{0:T(1024)} %mask_h.1, bf16[48,96,128]{2,1,0:T(8,128)(2,1)} %pair.1, s32[48,96]{1,0:T(8,128)} %bins_h.1, bf16[15,128]{1,0:T(8,128)(2,1)} %emb.1, f32[1,128]{1,0:T(1,128)} %bitcast.6, f32[1,128]{1,0:T(1,128)} %bitcast.7, ...), custom_call_target="tpu_custom_call" | custom-call | tf_op jit(solution)/shard_map/project/pallas_call | solution.py:170
  3.8 44.7 %all_to_all.10.recv = bf16[128,72,128]{2,1,0:T(8,128)(2,1)S(1)} all-to-all(bf16[128,72,128]{2,1,0:T(8,128)(2,1)S(1)} %get-tuple-element.8), channel_id=1, replica_groups=mesh['row'=16,'col'=8] {'row','col'}, dimensions={0} | all-to-all | bytes 4718592 | tf_op jit(solution)/shard_map/all_to_all | solution.py:341
  48.5 2.4 %triangle.1 = bf16[128,4,1152]{2,1,0:T(4,128)(2,1)S(1)} custom-call(bf16[128,72,128]{2,1,0:T(8,128)(2,1)S(1)} %all_to_all.10.recv), custom_call_target="tpu_custom_call" | custom-call | tf_op jit(solution)/shard_map/triangle/pallas_call | solution.py:250
  50.9 0.0 copy-start
  50.9 0.0 copy-start.1
  50.9 0.0 copy-start.2
  50.9 0.0 copy-start.3
  50.9 0.0 copy-start.4
  50.9 0.0 copy-start.5
  51.0 25.1 %all_to_all.11.tri = bf16[128,4,1152]{2,1,0:T(4,128)(2,1)S(1)} all-to-all(bf16[128,4,1152]{2,1,0:T(4,128)(2,1)S(1)} %triangle.1), channel_id=1, replica_groups=mesh['row'=16,'col'=8] {'row','col'}, dimensions={0} | all-to-all | bytes 2359296 | tf_op jit(solution)/shard_map/all_to_all | solution.py:342
  76.0 0.0 copy-done
  76.0 0.0 copy-done.1
  76.0 0.0 copy-done.2
  76.0 0.0 copy-done.3
  76.0 0.0 copy-done.4
  76.1 0.0 copy-done.5
  76.1 3.0 %update.1 = bf16[48,96,128]{2,1,0:T(8,128)(2,1)} custom-call(bf16[128,4,1152]{2,1,0:T(4,128)(2,1)S(1)} %all_to_all.11.tri, bf16[128,4608]{1,0:T(8,128)(2,1)S(1)} %get-tuple-element.9.normed, s32[3,12,128]{2,1,0:T(8,128)S(1)} %get-tuple-element.10.codes, bf16[48,96,128]{2,1,0:T(8,128)(2,1)S(1)} %copy-done, bf16[15,128]{1,0:T(8,128)(2,1)S(1)} %copy-done.3, ...), custom_call_target="tpu_custom_call" | custom-call | tf_op jit(solution)/shard_map/update/pallas_call | solution.py:309
Async XLA Ops:
  50.9 25.1 %copy-start = (bf16[48,96,128]{2,1,0:T(8,128)(2,1)S(1)}, bf16[48,96,128]{2,1,0:T(8,128)(2,1)}, u32[]{:S(2)}) copy-start(bf16[48,96,128]{2,1,0:T(8,128)(2,1)} %pair.1) | copy-start | bytes 3538948
  50.9 25.1 %copy-start.1 = (bf16[128,128]{1,0:T(8,128)(2,1)S(1)}, bf16[128,128]{1,0:T(8,128)(2,1)}, u32[]{:S(2)}) copy-start(bf16[128,128]{1,0:T(8,128)(2,1)} %gate_weight.1) | copy-start | bytes 98308
  50.9 25.1 %copy-start.2 = (bf16[128,128]{1,0:T(8,128)(2,1)S(1)}, bf16[128,128]{1,0:T(8,128)(2,1)}, u32[]{:S(2)}) copy-start(bf16[128,128]{1,0:T(8,128)(2,1)} %out_weight.1) | copy-start | bytes 98308
  50.9 25.1 %copy-start.3 = (bf16[15,128]{1,0:T(8,128)(2,1)S(1)}, bf16[15,128]{1,0:T(8,128)(2,1)}, u32[]{:S(2)}) copy-start(bf16[15,128]{1,0:T(8,128)(2,1)} %emb.1) | copy-start | bytes 11524
  50.9 25.1 %copy-start.4 = (f32[128]{0:T(128)S(1)}, f32[128]{0:T(128)}, u32[]{:S(2)}) copy-start(f32[128]{0:T(128)} %param.19) | copy-start | bytes 1540
  50.9 25.1 %copy-start.5 = (f32[128]{0:T(128)S(1)}, f32[128]{0:T(128)}, u32[]{:S(2)}) copy-start(f32[128]{0:T(128)} %param.20) | copy-start | bytes 1540

commit v2 on v1

--- a/solution.py
+++ b/solution.py
@@ -211,7 +211,7 @@
             src = []
             for z in range(4):
                 q, m = divmod(4 * tile + z, 3)
-                src.append(recv[8 * r + q, 24 * m : 24 * (m + 1)].astype(F32))
+                src.append(recv[16 * q + r, 24 * m : 24 * (m + 1)].astype(F32))
             got = []
             for h, e in places:
                 merged = pick((slot + 4 - e) % 4, [v[8 * h : 8 * (h + 1)] for v in src])
@@ -236,7 +236,7 @@
             heads = [full[3 * q + m] for m in range(3)]
             parts = [v[at : at + 4] for v in heads for at in (0, 4)]
             parts += [ends[3 * q + m] for m in range(3)]
-            out[8 * r + q] = jnp.concatenate(parts, axis=1).astype(BF16)
+            out[16 * q + r] = jnp.concatenate(parts, axis=1).astype(BF16)
 
     for r in range(16):
         gather(r, RIGHT_AT, right)
@@ -338,8 +338,8 @@
     sides, normed, codes = project(
         mask, pair, bins, emb_table, row(ln_gain), row(ln_bias), proj_weight
     )
-    recv = lax.all_to_all(sides, ("row", "col"), 0, 0, tiled=True)
-    tri = lax.all_to_all(triangle(recv), ("row", "col"), 0, 0, tiled=True)
+    recv = lax.all_to_all(sides, ("col", "row"), 0, 0, tiled=True)
+    tri = lax.all_to_all(triangle(recv), ("col", "row"), 0, 0, tiled=True)
     return update(
         tri, normed, codes, pair, emb_table, row(norm_gain), row(norm_bias), gate_weight, out_weight
     )

time: 79.2 us -> 78.5 us (level)
  no operation moved by 1% of the time
where the time goes in v2:
time: 78.5 us; the launch traced here: 78.4 us
  blocking collectives  69.1 us (88%)
  Pallas kernels  9.13 us (12%)
    all_to_all x1, blocking collectives, body(): recv = lax.all_to_all(sides, ('col', 'row'), 0, 0, tiled=True)  43.9 us
    all_to_all x1, blocking collectives, body(): tri = lax.all_to_all(triangle(recv), ('col', 'row'), 0, 0, tiled=True)  25.2 us
    pallas_call x1, Pallas kernels, project(): pl.pallas_call(project_kernel, in_specs=[IN_HBM] * 7, out_specs=[IN_VMEM]...  3.77 us
    pallas_call x1, Pallas kernels, update(): pl.pallas_call(update_kernel, in_specs=[IN_VMEM] * 9, out_specs=IN_HBM, o...  2.99 us
    pallas_call x1, Pallas kernels, triangle(): pl.pallas_call(triangle_kernel, in_specs=[IN_VMEM], out_specs=IN_VMEM, ou...  2.37 us

profile of v2, /device:TPU:1, one launch (start us, length us, event | category | flops | bytes accessed | tf_op | source)
XLA Modules:
  0.0 78.4 jit_solution(8483647490648445062)
XLA Ops:
  0.0 3.8 %project.1 = (bf16[128,72,128]{2,1,0:T(8,128)(2,1)S(1)}, bf16[128,4608]{1,0:T(8,128)(2,1)S(1)}, s32[3,12,128]{2,1,0:T(8,128)S(1)}) custom-call(s32[768]{0:T(1024)} %mask_h.1, bf16[48,96,128]{2,1,0:T(8,128)(2,1)} %pair.1, s32[48,96]{1,0:T(8,128)} %bins_h.1, bf16[15,128]{1,0:T(8,128)(2,1)} %emb.1, f32[1,128]{1,0:T(1,128)} %bitcast.6, f32[1,128]{1,0:T(1,128)} %bitcast.7, ...), custom_call_target="tpu_custom_call" | custom-call | tf_op jit(solution)/shard_map/project/pallas_call | solution.py:170
  3.8 43.9 %all_to_all.10.recv = bf16[128,72,128]{2,1,0:T(8,128)(2,1)S(1)} all-to-all(bf16[128,72,128]{2,1,0:T(8,128)(2,1)S(1)} %get-tuple-element.8), channel_id=1, replica_groups=mesh['row'=16,'col'=8] {'col','row'}, dimensions={0} | all-to-all | bytes 4718592 | tf_op jit(solution)/shard_map/all_to_all | solution.py:341
  47.6 2.4 %triangle.1 = bf16[128,4,1152]{2,1,0:T(4,128)(2,1)S(1)} custom-call(bf16[128,72,128]{2,1,0:T(8,128)(2,1)S(1)} %all_to_all.10.recv), custom_call_target="tpu_custom_call" | custom-call | tf_op jit(solution)/shard_map/triangle/pallas_call | solution.py:250
  50.0 0.0 copy-start
  50.0 0.0 copy-start.1
  50.0 0.0 copy-start.2
  50.1 0.0 copy-start.3
  50.1 0.0 copy-start.4
  50.1 0.0 copy-start.5
  50.1 25.2 %all_to_all.11.tri = bf16[128,4,1152]{2,1,0:T(4,128)(2,1)S(1)} all-to-all(bf16[128,4,1152]{2,1,0:T(4,128)(2,1)S(1)} %triangle.1), channel_id=1, replica_groups=mesh['row'=16,'col'=8] {'col','row'}, dimensions={0} | all-to-all | bytes 2359296 | tf_op jit(solution)/shard_map/all_to_all | solution.py:342
  75.3 0.0 copy-done
  75.3 0.0 copy-done.1
  75.3 0.0 copy-done.2
  75.4 0.0 copy-done.3
  75.4 0.0 copy-done.4
  75.4 0.0 copy-done.5
  75.4 3.0 %update.1 = bf16[48,96,128]{2,1,0:T(8,128)(2,1)} custom-call(bf16[128,4,1152]{2,1,0:T(4,128)(2,1)S(1)} %all_to_all.11.tri, bf16[128,4608]{1,0:T(8,128)(2,1)S(1)} %get-tuple-element.9.normed, s32[3,12,128]{2,1,0:T(8,128)S(1)} %get-tuple-element.10.codes, bf16[48,96,128]{2,1,0:T(8,128)(2,1)S(1)} %copy-done, bf16[15,128]{1,0:T(8,128)(2,1)S(1)} %copy-done.3, ...), custom_call_target="tpu_custom_call" | custom-call | tf_op jit(solution)/shard_map/update/pallas_call | solution.py:309
Async XLA Ops:
  50.0 25.3 %copy-start = (bf16[48,96,128]{2,1,0:T(8,128)(2,1)S(1)}, bf16[48,96,128]{2,1,0:T(8,128)(2,1)}, u32[]{:S(2)}) copy-start(bf16[48,96,128]{2,1,0:T(8,128)(2,1)} %pair.1) | copy-start | bytes 3538948
  50.0 25.3 %copy-start.1 = (bf16[128,128]{1,0:T(8,128)(2,1)S(1)}, bf16[128,128]{1,0:T(8,128)(2,1)}, u32[]{:S(2)}) copy-start(bf16[128,128]{1,0:T(8,128)(2,1)} %gate_weight.1) | copy-start | bytes 98308
  50.0 25.3 %copy-start.2 = (bf16[128,128]{1,0:T(8,128)(2,1)S(1)}, bf16[128,128]{1,0:T(8,128)(2,1)}, u32[]{:S(2)}) copy-start(bf16[128,128]{1,0:T(8,128)(2,1)} %out_weight.1) | copy-start | bytes 98308
  50.1 25.3 %copy-start.3 = (bf16[15,128]{1,0:T(8,128)(2,1)S(1)}, bf16[15,128]{1,0:T(8,128)(2,1)}, u32[]{:S(2)}) copy-start(bf16[15,128]{1,0:T(8,128)(2,1)} %emb.1) | copy-start | bytes 11524
  50.1 25.3 %copy-start.4 = (f32[128]{0:T(128)S(1)}, f32[128]{0:T(128)}, u32[]{:S(2)}) copy-start(f32[128]{0:T(128)} %param.19) | copy-start | bytes 1540
  50.1 25.3 %copy-start.5 = (f32[128]{0:T(128)S(1)}, f32[128]{0:T(128)}, u32[]{:S(2)}) copy-start(f32[128]{0:T(128)} %param.20) | copy-start | bytes 1540

commit v3 on v2

--- a/solution.py
+++ b/solution.py
@@ -68,6 +68,31 @@
     return jnp.concatenate([emb.astype(F32), jnp.zeros((1, 128), F32)], axis=0)
 
 
+def gate_weights(gate_weight, emb):
+    zeros = jnp.zeros((128, 128), BF16)
+    gate = jnp.concatenate([(0.5 * gate_weight.astype(F32)).astype(BF16), zeros], axis=1)
+    return jnp.concatenate(
+        [gate, jnp.concatenate([zeros[:16], padded(emb).astype(BF16)], axis=1)], axis=0
+    )
+
+
+def gate_and_total(m, rot, normed, codes, pair, weights):
+    hot = one_hot(jnp.concatenate([codes[m, c : c + 1, :] for c in range(12)], axis=1))
+    lanes = slice(1536 * m, 1536 * (m + 1))
+    mixed = dot(jnp.concatenate([normed[:, lanes], hot], axis=0), weights, TN)
+    rows = [
+        pair[column_row(c, (s + 4 - rot) % 4), 32 * m : 32 * m + 32]
+        for c in range(12)
+        for s in range(4)
+    ]
+    gate = 0.5 * jnp.tanh(mixed[:, :128]) + 0.5
+    return gate, jnp.concatenate(rows, axis=0).astype(F32) + mixed[:, 128:]
+
+
+def ahead(q):
+    return q % 2 == 0
+
+
 def columns(codes, shift, rot):
     entry = (lanes_slot((8, 128)) + 4 - rot) % 4
     turn = lambda x, e: pltpu.roll(x, 32 * ((e + shift) % 4), 1)
@@ -87,20 +112,21 @@
 
 
 def project_kernel(
-    mask_h, pair_h, bins_h, emb_h, gain_h, bias_h, weight_h, out, normed_out, codes_out,
-    mask, pair, bins, emb, gain, bias, weight, code, normed, done, sems,
+    mask_h, pair_h, bins_h, emb_h, gain_h, bias_h, weight_h, gate_weight_h,
+    out, normed_out, codes_out, gate_out, total_out,
+    mask, pair, bins, emb, gain, bias, weight, gate_weight, code, normed, done, sems,
 ):
     r, q = lax.axis_index("row"), lax.axis_index("col")
     small = [
         pltpu.make_async_copy(a, b, sems.at[n])
         for n, (a, b) in enumerate(
-            ((mask_h, mask), (weight_h, weight), (gain_h, gain), (bias_h, bias), (emb_h, emb), (bins_h, bins))
+            ((mask_h, mask), (weight_h, weight), (gain_h, gain), (bias_h, bias), (emb_h, emb), (bins_h, bins), (gate_weight_h, gate_weight))
         )
     ]
     large = []
     for m in range(3):
         at = (slice(None), pl.ds(32 * m, 32))
-        large.append(pltpu.make_async_copy(pair_h.at[at], pair.at[at], sems.at[6 + m]))
+        large.append(pltpu.make_async_copy(pair_h.at[at], pair.at[at], sems.at[7 + m]))
     for copy in small + large:
         copy.start()
     for copy in small[:4]:
@@ -165,16 +191,27 @@
             done[24 * m + 16 + g] = jnp.where(low, right_end, right[:, own]).astype(BF16)
     out[...] = jnp.swapaxes(done[...], 0, 1)
 
-
-def project(mask, pair, bins, emb, gain, bias, weight):
+    @pl.when(ahead(q))
+    def _():
+        weights = gate_weights(gate_weight[...], emb[...])
+        for m in range(3):
+            lanes = slice(1536 * m, 1536 * (m + 1))
+            gate_out[lanes], total_out[lanes] = gate_and_total(
+                m, (3 * q + m) % 4, normed_out, codes_out, pair, weights
+            )
+
+
+def project(*args):
     return pl.pallas_call(
         project_kernel,
-        in_specs=[IN_HBM] * 7,
-        out_specs=[IN_VMEM] * 3,
+        in_specs=[IN_HBM] * 8,
+        out_specs=[IN_VMEM] * 5,
         out_shape=[
             jax.ShapeDtypeStruct((128, 72, 128), BF16),
             jax.ShapeDtypeStruct((128, 4608), BF16),
             jax.ShapeDtypeStruct((3, 12, 128), I32),
+            jax.ShapeDtypeStruct((4608, 128), F32),
+            jax.ShapeDtypeStruct((4608, 128), F32),
         ],
         scratch_shapes=[
             pltpu.SMEM((768,), I32),
@@ -184,14 +221,15 @@
             pltpu.VMEM((1, 128), F32),
             pltpu.VMEM((1, 128), F32),
             pltpu.VMEM((128, 512), BF16),
+            pltpu.VMEM((128, 128), BF16),
             pltpu.VMEM((48, 128), I32),
             pltpu.VMEM((128, 4608), BF16),
             pltpu.VMEM((72, 128, 128), BF16),
-            pltpu.SemaphoreType.DMA((9,)),
+            pltpu.SemaphoreType.DMA((10,)),
         ],
         compiler_params=pltpu.CompilerParams(vmem_limit_bytes=LIMIT),
         name="project",
-    )(*in_hbm(mask, pair, bins, emb, gain, bias, weight))
+    )(*in_hbm(*args))
 
 
 LEFT_AT = [(0, 0), (0, 1), (0, 2), (0, 3), (1, 2), (1, 3)]
@@ -263,44 +301,50 @@
 
 
 def update_kernel(
-    tri, normed, codes, pair, emb, gain, bias, gate_weight, out_weight, out, sums, result, sems
+    tri, normed, codes, gate_in, total_in, pair, emb, gain, bias, gate_weight, out_weight, out,
+    sums, result, sems,
 ):
     q = lax.axis_index("col")
-    gain_t, bias_t = down(gain[...]), down(bias[...])
-    zeros = jnp.zeros((128, 128), BF16)
-    both = jnp.concatenate(
-        [
-            jnp.concatenate([(0.5 * gate_weight[...].astype(F32)).astype(BF16), zeros], axis=1),
-            jnp.concatenate([zeros[:16], padded(emb[...]).astype(BF16)], axis=1),
-        ],
-        axis=0,
-    )
-    for u in range(9):
-        part = tri[:, :, 128 * u : 128 * (u + 1)].astype(F32)
-        sums[512 * u : 512 * (u + 1)] = part.reshape(512, 128)
-    stores = []
-    for m in range(3):
-        rot = (3 * q + m) % 4
-        at = slice(32 * m, 32 * m + 32)
-        hot = one_hot(jnp.concatenate([codes[m, c : c + 1, :] for c in range(12)], axis=1))
-        lanes = slice(1536 * m, 1536 * (m + 1))
-        mixed = dot(jnp.concatenate([normed[:, lanes], hot], axis=0), both, TN)
-        x = []
-        for c in range(12):
-            u, v = divmod(8 * m + c if c < 8 else 16 + 4 * m + c, 4)
-            x.append(sums[pl.ds(512 * u + v, 128, stride=4), :])
-        tri_normed = norm_sublanes(jnp.concatenate(x, axis=1), gain_t, bias_t)
-        change = dot(jnp.concatenate(tri_normed, axis=1).astype(BF16), out_weight[...], TN)
-        change = (0.5 * jnp.tanh(mixed[:, :128]) + 0.5) * change
-        for c in range(12):
-            for s in range(4):
-                i = column_row(c, (s + 4 - rot) % 4)
-                k = slice(128 * c + 32 * s, 128 * c + 32 * s + 32)
-                total = pair[i, at].astype(F32) + mixed[k, 128:]
-                result[i, at] = (total + change[k]).astype(BF16)
-        part = (slice(None), pl.ds(32 * m, 32))
-        stores.append(pltpu.make_async_copy(result.at[part], out.at[part], sems.at[m]))
-        stores[m].start()
+    stores = [
+        pltpu.make_async_copy(result.at[part], out.at[part], sems.at[m])
+        for m, part in enumerate([(slice(None), pl.ds(32 * m, 32)) for m in range(3)])
+    ]
+
+    def finish(gates):
+        gain_t, bias_t = down(gain[...]), down(bias[...])
+        for u in range(9):
+            part = tri[:, :, 128 * u : 128 * (u + 1)].astype(F32)
+            sums[512 * u : 512 * (u + 1)] = part.reshape(512, 128)
+        for m in range(3):
+            rot = (3 * q + m) % 4
+            gate, total = gates(m, rot)
+            x = []
+            for c in range(12):
+                u, v = divmod(8 * m + c if c < 8 else 16 + 4 * m + c, 4)
+                x.append(sums[pl.ds(512 * u + v, 128, stride=4), :])
+            tri_normed = norm_sublanes(jnp.concatenate(x, axis=1), gain_t, bias_t)
+            tri_normed = jnp.concatenate(tri_normed, axis=1).astype(BF16)
+            new = total + gate * dot(tri_normed, out_weight[...], TN)
+            for c in range(12):
+                for s in range(4):
+                    k = 128 * c + 32 * s
+                    i = column_row(c, (s + 4 - rot) % 4)
+                    result[i, 32 * m : 32 * m + 32] = new[k : k + 32].astype(BF16)
+            stores[m].start()
+
+    @pl.when(ahead(q))
+    def _():
+        def gates(m, rot):
+            lanes = slice(1536 * m, 1536 * (m + 1))
+            return gate_in[lanes], total_in[lanes]
+
+        finish(gates)
+
+    @pl.when(jnp.logical_not(ahead(q)))
+    def _():
+        weights = gate_weights(gate_weight[...], emb[...])
+        finish(lambda m, rot: gate_and_total(m, rot, normed, codes, pair, weights))
+
     for store in stores:
         store.wait()
 
@@ -308,7 +352,7 @@
 def update(*args):
     return pl.pallas_call(
         update_kernel,
-        in_specs=[IN_VMEM] * 9,
+        in_specs=[IN_VMEM] * 11,
         out_specs=IN_HBM,
         out_shape=jax.ShapeDtypeStruct((48, 96, 128), BF16),
         scratch_shapes=[
@@ -335,13 +379,13 @@
     out_weight,
 ):
     row = lambda v: v.reshape(1, 128)
-    sides, normed, codes = project(
-        mask, pair, bins, emb_table, row(ln_gain), row(ln_bias), proj_weight
+    sides, *kept = project(
+        mask, pair, bins, emb_table, row(ln_gain), row(ln_bias), proj_weight, gate_weight
     )
     recv = lax.all_to_all(sides, ("col", "row"), 0, 0, tiled=True)
     tri = lax.all_to_all(triangle(recv), ("col", "row"), 0, 0, tiled=True)
     return update(
-        tri, normed, codes, pair, emb_table, row(norm_gain), row(norm_bias), gate_weight, out_weight
+        tri, *kept, pair, emb_table, row(norm_gain), row(norm_bias), gate_weight, out_weight
     )
 
 

time: 78.5 us -> 78.1 us (level)
  blocking collectives: 69.1 us -> 68.2 us
    all_to_all x1, blocking collectives: 43.9 us -> 43 us  [body(): recv = lax.all_to_all(sides, ('col', 'row'), 0, 0, tiled=True)]
where the time goes in v3:
time: 78.1 us; the launch traced here: 78 us
  blocking collectives  68.2 us (87%)
  Pallas kernels  9.62 us (12%)
    all_to_all x1, blocking collectives, body(): recv = lax.all_to_all(sides, ('col', 'row'), 0, 0, tiled=True)  43 us
    all_to_all x1, blocking collectives, body(): tri = lax.all_to_all(triangle(recv), ('col', 'row'), 0, 0, tiled=True)  25.2 us
    pallas_call x1, Pallas kernels, project(): pl.pallas_call(project_kernel, in_specs=[IN_HBM] * 8, out_specs=[IN_VMEM]...  4.7 us
    pallas_call x1, Pallas kernels, update(): pl.pallas_call(update_kernel, in_specs=[IN_VMEM] * 11, out_specs=IN_HBM,...  2.55 us
    pallas_call x1, Pallas kernels, triangle(): pl.pallas_call(triangle_kernel, in_specs=[IN_VMEM], out_specs=IN_VMEM, ou...  2.37 us

profile of v3, /device:TPU:1, one launch (start us, length us, event | category | flops | bytes accessed | tf_op | source)
XLA Modules:
  0.0 78.0 jit_solution(9246821122492268629)
XLA Ops:
  0.0 4.7 %project.1 = (bf16[128,72,128]{2,1,0:T(8,128)(2,1)S(1)}, bf16[128,4608]{1,0:T(8,128)(2,1)S(1)}, s32[3,12,128]{2,1,0:T(8,128)S(1)}, f32[4608,128]{1,0:T(8,128)S(1)}, f32[4608,128]{1,0:T(8,128)S(1)}) custom-call(s32[768]{0:T(1024)} %mask_h.1, bf16[48,96,128]{2,1,0:T(8,128)(2,1)} %pair.1, s32[48,96]{1,0:T(8,128)} %bins_h.1, bf16[15,128]{1,0:T(8,128)(2,1)} %emb.1, ...), custom_call_target="tpu_custom_call" | custom-call | tf_op jit(solution)/shard_map/project/pallas_call | solution.py:205
  4.7 43.0 %all_to_all.10.recv = bf16[128,72,128]{2,1,0:T(8,128)(2,1)S(1)} all-to-all(bf16[128,72,128]{2,1,0:T(8,128)(2,1)S(1)} %get-tuple-element.10), channel_id=1, replica_groups=mesh['row'=16,'col'=8] {'col','row'}, dimensions={0} | all-to-all | bytes 4718592 | tf_op jit(solution)/shard_map/all_to_all | solution.py:385
  47.7 2.4 %triangle.1 = bf16[128,4,1152]{2,1,0:T(4,128)(2,1)S(1)} custom-call(bf16[128,72,128]{2,1,0:T(8,128)(2,1)S(1)} %all_to_all.10.recv), custom_call_target="tpu_custom_call" | custom-call | tf_op jit(solution)/shard_map/triangle/pallas_call | solution.py:288
  50.1 0.0 copy-start
  50.1 0.0 copy-start.1
  50.1 0.0 copy-start.2
  50.1 0.0 copy-start.3
  50.1 0.0 copy-start.4
  50.1 0.0 copy-start.5
  50.1 25.2 %all_to_all.11.tri = bf16[128,4,1152]{2,1,0:T(4,128)(2,1)S(1)} all-to-all(bf16[128,4,1152]{2,1,0:T(4,128)(2,1)S(1)} %triangle.1), channel_id=1, replica_groups=mesh['row'=16,'col'=8] {'col','row'}, dimensions={0} | all-to-all | bytes 2359296 | tf_op jit(solution)/shard_map/all_to_all | solution.py:386
  75.4 0.0 copy-done
  75.4 0.0 copy-done.1
  75.4 0.0 copy-done.2
  75.4 0.0 copy-done.3
  75.4 0.0 copy-done.4
  75.4 0.0 copy-done.5
  75.4 2.6 %update.1 = bf16[48,96,128]{2,1,0:T(8,128)(2,1)} custom-call(bf16[128,4,1152]{2,1,0:T(4,128)(2,1)S(1)} %all_to_all.11.tri, bf16[128,4608]{1,0:T(8,128)(2,1)S(1)} %get-tuple-element.11.normed, s32[3,12,128]{2,1,0:T(8,128)S(1)} %get-tuple-element.12.codes, f32[4608,128]{1,0:T(8,128)S(1)} %get-tuple-element.13.gate_in, ...), custom_call_target="tpu_custom_call" | custom-call | tf_op jit(solution)/shard_map/update/pallas_call | solution.py:353
Async XLA Ops:
  50.1 25.3 %copy-start = (bf16[48,96,128]{2,1,0:T(8,128)(2,1)S(1)}, bf16[48,96,128]{2,1,0:T(8,128)(2,1)}, u32[]{:S(2)}) copy-start(bf16[48,96,128]{2,1,0:T(8,128)(2,1)} %pair.1) | copy-start | bytes 3538948
  50.1 25.3 %copy-start.1 = (bf16[128,128]{1,0:T(8,128)(2,1)S(1)}, bf16[128,128]{1,0:T(8,128)(2,1)}, u32[]{:S(2)}) copy-start(bf16[128,128]{1,0:T(8,128)(2,1)} %gate_weight.1) | copy-start | bytes 98308
  50.1 25.3 %copy-start.2 = (bf16[128,128]{1,0:T(8,128)(2,1)S(1)}, bf16[128,128]{1,0:T(8,128)(2,1)}, u32[]{:S(2)}) copy-start(bf16[128,128]{1,0:T(8,128)(2,1)} %out_weight.1) | copy-start | bytes 98308
  50.1 25.3 %copy-start.3 = (bf16[15,128]{1,0:T(8,128)(2,1)S(1)}, bf16[15,128]{1,0:T(8,128)(2,1)}, u32[]{:S(2)}) copy-start(bf16[15,128]{1,0:T(8,128)(2,1)} %emb.1) | copy-start | bytes 11524
  50.1 25.3 %copy-start.4 = (f32[128]{0:T(128)S(1)}, f32[128]{0:T(128)}, u32[]{:S(2)}) copy-start(f32[128]{0:T(128)} %param.19) | copy-start | bytes 1540
  50.1 25.3 %copy-start.5 = (f32[128]{0:T(128)S(1)}, f32[128]{0:T(128)}, u32[]{:S(2)}) copy-start(f32[128]{0:T(128)} %param.20) | copy-start | bytes 1540

commit v4 on v3

--- a/solution.py
+++ b/solution.py
@@ -12,6 +12,8 @@
 NT = (((1,), (1,)), ((), ()))
 TN = (((0,), (0,)), ((), ()))
 NN = (((1,), (0,)), ((), ()))
+ROW, COL = ("y", "z_lo", "core"), ("x", "z_hi")
+CORE_FIRST = ("core", "y", "z_lo", "x", "z_hi")
 LIMIT = 24 * 1024 * 1024
 IN_HBM = pl.BlockSpec(memory_space=pltpu.HBM)
 IN_VMEM = pl.BlockSpec(memory_space=pltpu.VMEM)
@@ -89,6 +91,14 @@
     return gate, jnp.concatenate(rows, axis=0).astype(F32) + mixed[:, 128:]
 
 
+def place_row():
+    return 4 * lax.axis_index("y") + 2 * lax.axis_index("z_lo") + lax.axis_index("core")
+
+
+def place_col():
+    return 2 * lax.axis_index("x") + lax.axis_index("z_hi")
+
+
 def ahead(q):
     return q % 2 == 0
 
@@ -116,7 +126,7 @@
     out, normed_out, codes_out, gate_out, total_out,
     mask, pair, bins, emb, gain, bias, weight, gate_weight, code, normed, done, sems,
 ):
-    r, q = lax.axis_index("row"), lax.axis_index("col")
+    r, q = place_row(), place_col()
     small = [
         pltpu.make_async_copy(a, b, sems.at[n])
         for n, (a, b) in enumerate(
@@ -249,7 +259,7 @@
             src = []
             for z in range(4):
                 q, m = divmod(4 * tile + z, 3)
-                src.append(recv[16 * q + r, 24 * m : 24 * (m + 1)].astype(F32))
+                src.append(recv[64 * (r % 2) + 8 * (r // 2) + q, 24 * m : 24 * (m + 1)].astype(F32))
             got = []
             for h, e in places:
                 merged = pick((slot + 4 - e) % 4, [v[8 * h : 8 * (h + 1)] for v in src])
@@ -274,7 +284,7 @@
             heads = [full[3 * q + m] for m in range(3)]
             parts = [v[at : at + 4] for v in heads for at in (0, 4)]
             parts += [ends[3 * q + m] for m in range(3)]
-            out[16 * q + r] = jnp.concatenate(parts, axis=1).astype(BF16)
+            out[64 * (r % 2) + 8 * (r // 2) + q] = jnp.concatenate(parts, axis=1).astype(BF16)
 
     for r in range(16):
         gather(r, RIGHT_AT, right)
@@ -304,7 +314,7 @@
     tri, normed, codes, gate_in, total_in, pair, emb, gain, bias, gate_weight, out_weight, out,
     sums, result, sems,
 ):
-    q = lax.axis_index("col")
+    q = place_col()
     stores = [
         pltpu.make_async_copy(result.at[part], out.at[part], sems.at[m])
         for m, part in enumerate([(slice(None), pl.ds(32 * m, 32)) for m in range(3)])
@@ -382,15 +392,16 @@
     sides, *kept = project(
         mask, pair, bins, emb_table, row(ln_gain), row(ln_bias), proj_weight, gate_weight
     )
-    recv = lax.all_to_all(sides, ("col", "row"), 0, 0, tiled=True)
-    tri = lax.all_to_all(triangle(recv), ("col", "row"), 0, 0, tiled=True)
+    recv = lax.all_to_all(sides, CORE_FIRST, 0, 0, tiled=True)
+    tri = lax.all_to_all(triangle(recv), CORE_FIRST, 0, 0, tiled=True)
     return update(
         tri, *kept, pair, emb_table, row(norm_gain), row(norm_bias), gate_weight, out_weight
     )
 
 
 def solution(mesh):
-    placed = (P("row", "col", None), P("row", "col"), P(), P(), P(), P(), P(), P(), P(), P(), P())
+    parts = jax.sharding.Mesh(mesh.devices.reshape(4, 2, 2, 4, 2), ROW + COL)
+    placed = (P(ROW, COL, None), P(ROW, COL), P(), P(), P(), P(), P(), P(), P(), P(), P())
     return jax.shard_map(
-        body, mesh=mesh, in_specs=placed, out_specs=P("row", "col", None), check_vma=False
+        body, mesh=parts, in_specs=placed, out_specs=P(ROW, COL, None), check_vma=False
     )

time: 78.1 us -> 79.3 us (1.015)
  blocking collectives: 68.2 us -> 69.3 us
    all_to_all x2, blocking collectives: 68.2 us -> 69.3 us  [the longest x1 42.8 us: body(): recv = lax.all_to_all(sides, CORE_FIRST, 0, 0, tiled=True)]
where the time goes in v4:
time: 79.3 us; the launch traced here: 79.1 us
  blocking collectives  69.3 us (87%)
  Pallas kernels  9.63 us (12%)
    all_to_all x1, blocking collectives, body(): recv = lax.all_to_all(sides, CORE_FIRST, 0, 0, tiled=True)  42.8 us
    all_to_all x1, blocking collectives, body(): tri = lax.all_to_all(triangle(recv), CORE_FIRST, 0, 0, tiled=True)  26.6 us
    pallas_call x1, Pallas kernels, project(): pl.pallas_call(project_kernel, in_specs=[IN_HBM] * 8, out_specs=[IN_VMEM]...  4.7 us
    pallas_call x1, Pallas kernels, update(): pl.pallas_call(update_kernel, in_specs=[IN_VMEM] * 11, out_specs=IN_HBM,...  2.56 us
    pallas_call x1, Pallas kernels, triangle(): pl.pallas_call(triangle_kernel, in_specs=[IN_VMEM], out_specs=IN_VMEM, ou...  2.38 us

profile of v4, /device:TPU:1, one launch (start us, length us, event | category | flops | bytes accessed | tf_op | source)
XLA Modules:
  0.0 79.1 jit_solution(1617499465996461055)
XLA Ops:
  0.0 4.7 %project.1 = (bf16[128,72,128]{2,1,0:T(8,128)(2,1)S(1)}, bf16[128,4608]{1,0:T(8,128)(2,1)S(1)}, s32[3,12,128]{2,1,0:T(8,128)S(1)}, f32[4608,128]{1,0:T(8,128)S(1)}, f32[4608,128]{1,0:T(8,128)S(1)}) custom-call(s32[768]{0:T(1024)} %mask_h.1, bf16[48,96,128]{2,1,0:T(8,128)(2,1)} %pair.1, s32[48,96]{1,0:T(8,128)} %bins_h.1, bf16[15,128]{1,0:T(8,128)(2,1)} %emb.1, ...), custom_call_target="tpu_custom_call" | custom-call | tf_op jit(solution)/shard_map/project/pallas_call | solution.py:215
  4.7 42.8 %all_to_all.10.recv = bf16[128,72,128]{2,1,0:T(8,128)(2,1)S(1)} all-to-all(bf16[128,72,128]{2,1,0:T(8,128)(2,1)S(1)} %get-tuple-element.10), channel_id=1, replica_groups=mesh['y'=4,'z_lo'=2,'core'=2,'x'=4,'z_hi'=2] {'core','y','z_lo','x','z_hi'}, dimensions={0} | all-to-all | bytes 4718592 | tf_op jit(solution)/shard_map/all_to_all | solution.py:395
  47.5 2.4 %triangle.1 = bf16[128,4,1152]{2,1,0:T(4,128)(2,1)S(1)} custom-call(bf16[128,72,128]{2,1,0:T(8,128)(2,1)S(1)} %all_to_all.10.recv), custom_call_target="tpu_custom_call" | custom-call | tf_op jit(solution)/shard_map/triangle/pallas_call | solution.py:298
  49.9 0.0 copy-start
  49.9 0.0 copy-start.1
  49.9 0.0 copy-start.2
  49.9 0.0 copy-start.3
  49.9 0.0 copy-start.4
  49.9 0.0 copy-start.5
  49.9 26.6 %all_to_all.11.tri = bf16[128,4,1152]{2,1,0:T(4,128)(2,1)S(1)} all-to-all(bf16[128,4,1152]{2,1,0:T(4,128)(2,1)S(1)} %triangle.1), channel_id=1, replica_groups=mesh['y'=4,'z_lo'=2,'core'=2,'x'=4,'z_hi'=2] {'core','y','z_lo','x','z_hi'}, dimensions={0} | all-to-all | bytes 2359296 | tf_op jit(solution)/shard_map/all_to_all | solution.py:396
  76.5 0.0 copy-done
  76.5 0.0 copy-done.1
  76.5 0.0 copy-done.2
  76.5 0.0 copy-done.3
  76.5 0.0 copy-done.4
  76.5 0.0 copy-done.5
  76.5 2.6 %update.1 = bf16[48,96,128]{2,1,0:T(8,128)(2,1)} custom-call(bf16[128,4,1152]{2,1,0:T(4,128)(2,1)S(1)} %all_to_all.11.tri, bf16[128,4608]{1,0:T(8,128)(2,1)S(1)} %get-tuple-element.11.normed, s32[3,12,128]{2,1,0:T(8,128)S(1)} %get-tuple-element.12.codes, f32[4608,128]{1,0:T(8,128)S(1)} %get-tuple-element.13.gate_in, ...), custom_call_target="tpu_custom_call" | custom-call | tf_op jit(solution)/shard_map/update/pallas_call | solution.py:363
Async XLA Ops:
  49.9 26.6 %copy-start = (bf16[48,96,128]{2,1,0:T(8,128)(2,1)S(1)}, bf16[48,96,128]{2,1,0:T(8,128)(2,1)}, u32[]{:S(2)}) copy-start(bf16[48,96,128]{2,1,0:T(8,128)(2,1)} %pair.1) | copy-start | bytes 3538948
  49.9 26.6 %copy-start.1 = (bf16[128,128]{1,0:T(8,128)(2,1)S(1)}, bf16[128,128]{1,0:T(8,128)(2,1)}, u32[]{:S(2)}) copy-start(bf16[128,128]{1,0:T(8,128)(2,1)} %gate_weight.1) | copy-start | bytes 98308
  49.9 26.6 %copy-start.2 = (bf16[128,128]{1,0:T(8,128)(2,1)S(1)}, bf16[128,128]{1,0:T(8,128)(2,1)}, u32[]{:S(2)}) copy-start(bf16[128,128]{1,0:T(8,128)(2,1)} %out_weight.1) | copy-start | bytes 98308
  49.9 26.6 %copy-start.3 = (bf16[15,128]{1,0:T(8,128)(2,1)S(1)}, bf16[15,128]{1,0:T(8,128)(2,1)}, u32[]{:S(2)}) copy-start(bf16[15,128]{1,0:T(8,128)(2,1)} %emb.1) | copy-start | bytes 11524
  49.9 26.6 %copy-start.4 = (f32[128]{0:T(128)S(1)}, f32[128]{0:T(128)}, u32[]{:S(2)}) copy-start(f32[128]{0:T(128)} %param.19) | copy-start | bytes 1540
  49.9 26.6 %copy-start.5 = (f32[128]{0:T(128)S(1)}, f32[128]{0:T(128)}, u32[]{:S(2)}) copy-start(f32[128]{0:T(128)} %param.20) | copy-start | bytes 1540
